TPU v7x, 128 devices: a whole 4x4x4 slice. The times are simulated.
128 devices in a mesh: row: 4 (over z), col: 32 (over x, y, core).
Axes of the slice: x: 4, y: 4, z: 4, core: 2. Of those that a mesh axis runs over, the one named last changes fastest.
Arguments:
- layer_input: bfloat16 [1088, 16384], P('col', 'row'), may hold values from -6 to 6
- cotangent: bfloat16 [1088, 16384], P('col', 'row'), may hold values from -6 to 6
- segments: int32 [16, 1024], P('row'), may hold values from 0 to 3, as said below
- qkv_weight: bfloat16 [1088, 3, 1088], P('row', None, 'col'), may hold values from -0.1875 to 0.1875
- qv_bias: bfloat16 [2, 1088], P(None, 'col'), may hold values from -1 to 1
- out_weight: bfloat16 [1088, 1088], P('row', 'col'), may hold values from -1.5 to 1.5
- out_bias: bfloat16 [1088], P('col'), may hold values from -1 to 1
- up_weight: bfloat16 [1088, 4352], P('row', 'col'), may hold values from -0.1875 to 0.1875
- up_bias: bfloat16 [4352], P('col'), may hold values from -1 to 1
- down_weight: bfloat16 [4352, 1088], P('col', 'row'), may hold values from -0.09375 to 0.09375
- down_bias: bfloat16 [1088], P('col'), may hold values from -1 to 1
- first_gain: bfloat16 [1088], P('col'), may hold values from 0.5 to 1.5
- first_shift: bfloat16 [1088], P('col'), may hold values from -1 to 1
- second_gain: bfloat16 [1088], P('col'), may hold values from 0.5 to 1.5
- second_shift: bfloat16 [1088], P('col'), may hold values from -1 to 1
Outputs:
- layer_output: float32 [1088, 16384], P('col', 'row')
- input_grad: float32 [1088, 16384], P('col', 'row')
- qkv_grad: float32 [1088, 3, 1088], P('row', None, 'col')
- qvbias_grad: float32 [2, 1088], P(None, 'col')
- out_grad: float32 [1088, 1088], P('row', 'col')
- outbias_grad: float32 [1088], P('col')
- up_grad: float32 [1088, 4352], P('row', 'col')
- upbias_grad: float32 [4352], P('col')
- down_grad: float32 [4352, 1088], P('col', 'row')
- downbias_grad: float32 [1088], P('col')
- firstgain_grad: float32 [1088], P('col')
- firstshift_grad: float32 [1088], P('col')
- secondgain_grad: float32 [1088], P('col')
- secondshift_grad: float32 [1088], P('col')
Inputs may be any that keep to these rules, and one draw needn't show every extreme that they name: `segments`: segment numbers never fall along a sequence. In each row index's 4 sequences one sequence is a single document.
All inputs are finite; a program needn't handle non-finite values.
Results may differ from a plain program's by a relative error of at most 0.014.
Values may be sent and summed in bfloat16 or wider, within the bound.
A program may use at most 256 MiB of HBM per device.

v0:
```python
import jax
import jax.numpy as jnp
from jax import lax
from jax.sharding import PartitionSpec as P

HEADS = 17


epsilon = 1e-05


def for_sending(x):
    return jax.tree.map(lambda a: a.astype(jnp.bfloat16) if a.dtype == jnp.float32 else a, x)


def norm_rows(rows_in, gain_row, shift_row):
    row_mean = jnp.mean(rows_in, -1, keepdims=True)
    centred = rows_in - row_mean
    inv_std = lax.rsqrt(jnp.mean(centred * centred, -1, keepdims=True) + epsilon)
    standard = centred * inv_std
    return (standard * gain_row + shift_row, standard, inv_std)


def norm_back(partial_value, standard, gain_row, inv_std, column, col_width):
    col_count = lax.axis_size("col")
    weighted = partial_value * gain_row
    first_sum = jnp.sum(weighted, -1)
    second_sum = jnp.sum(weighted * standard, -1)
    first_cols = jnp.broadcast_to(first_sum[:, None], (first_sum.shape[0], col_count))
    second_cols = jnp.broadcast_to(second_sum[:, None], (second_sum.shape[0], col_count))
    local_grad, first_total, second_total = (
        lax.psum_scatter(partial_value, "col", scatter_dimension=1, tiled=True),
        lax.psum_scatter(first_cols, "col", scatter_dimension=1, tiled=True),
        lax.psum_scatter(second_cols, "col", scatter_dimension=1, tiled=True),
    )
    full_width = partial_value.shape[1]
    standard_mine = lax.dynamic_slice_in_dim(standard, column * col_width, col_width, 1)
    gain_mine = lax.dynamic_slice_in_dim(gain_row, column * col_width, col_width, 0)
    input_part = inv_std * (
        gain_mine * local_grad
        - first_total / full_width
        - standard_mine * second_total / full_width
    )
    return (input_part, local_grad, standard_mine)


def block_mask(slot_segs, begin_row, block_rows):
    query_pos = begin_row + jnp.arange(block_rows)
    key_pos = jnp.arange(slot_segs.shape[0])
    query_segs = slot_segs[begin_row : begin_row + block_rows]
    return (key_pos[None, :] <= query_pos[:, None]) & (slot_segs[None, :] == query_segs[:, None])


def slot_forward(slot_pair):
    slot_qkv, slot_segs = slot_pair
    query_rows = slot_qkv[:, 0]
    key_rows = slot_qkv[:, 1]
    value_rows = slot_qkv[:, 2]
    seq_len = slot_qkv.shape[0]
    block_rows = min(512, seq_len)
    scaling = query_rows.shape[-1] ** (-0.5)
    out_blocks = []
    lse_blocks = []
    for begin_row in range(0, seq_len, block_rows):
        scores = (
            jnp.einsum(
                "qd,kd->qk",
                query_rows[begin_row : begin_row + block_rows],
                key_rows,
                preferred_element_type=jnp.float32,
            )
            * scaling
        )
        scores = jnp.where(block_mask(slot_segs, begin_row, block_rows), scores, -1e30)
        row_max = jnp.max(scores, -1, keepdims=True)
        exponents = jnp.exp(scores - row_max)
        row_total = jnp.sum(exponents, -1, keepdims=True)
        weights = (exponents / row_total).astype(jnp.bfloat16)
        out_blocks.append(jnp.dot(weights, value_rows, preferred_element_type=jnp.float32))
        lse_blocks.append(row_max[:, 0] + jnp.log(row_total[:, 0]))
    return (jnp.concatenate(out_blocks, 0).astype(jnp.bfloat16), jnp.concatenate(lse_blocks, 0))


def slot_backward(slot_items):
    slot_qkv, slot_segs, slot_lse, slot_grad = slot_items
    query_rows = slot_qkv[:, 0]
    key_rows = slot_qkv[:, 1]
    value_rows = slot_qkv[:, 2]
    seq_len = slot_qkv.shape[0]
    block_rows = min(512, seq_len)
    scaling = query_rows.shape[-1] ** (-0.5)
    query_grads = []
    key_grad = jnp.zeros(key_rows.shape, jnp.float32)
    value_grad = jnp.zeros(value_rows.shape, jnp.float32)
    for begin_row in range(0, seq_len, block_rows):
        query_block = query_rows[begin_row : begin_row + block_rows]
        grad_block = slot_grad[begin_row : begin_row + block_rows]
        scores = (
            jnp.einsum("qd,kd->qk", query_block, key_rows, preferred_element_type=jnp.float32)
            * scaling
        )
        scores = jnp.where(block_mask(slot_segs, begin_row, block_rows), scores, -1e30)
        weights = jnp.exp(scores - slot_lse[begin_row : begin_row + block_rows, None])
        weights_low = weights.astype(jnp.bfloat16)
        grad_weights = jnp.einsum(
            "qd,kd->qk", grad_block, value_rows, preferred_element_type=jnp.float32
        )
        row_delta = jnp.sum(weights * grad_weights, -1, keepdims=True)
        grad_scores = (weights * (grad_weights - row_delta)).astype(jnp.bfloat16)
        query_grads.append(
            jnp.dot(grad_scores, key_rows, preferred_element_type=jnp.float32) * scaling
        )
        key_grad = (
            key_grad
            + jnp.einsum("qk,qd->kd", grad_scores, query_block, preferred_element_type=jnp.float32)
            * scaling
        )
        value_grad = value_grad + jnp.einsum(
            "qk,qd->kd", weights_low, grad_block, preferred_element_type=jnp.float32
        )
    return jnp.stack([jnp.concatenate(query_grads, 0), key_grad, value_grad], axis=1)


def shards(
    layer_input,
    cotangent,
    segments,
    qkv_weight,
    qv_bias,
    out_weight,
    out_bias,
    up_weight,
    up_bias,
    down_weight,
    down_bias,
    first_gain,
    first_shift,
    second_gain,
    second_shift,
):
    column = lax.axis_index("col")
    col_count = lax.axis_size("col")
    col_width = layer_input.shape[0]
    tok_rows = layer_input.shape[1]
    seq_count = segments.shape[0]
    seq_len = segments.shape[1]
    heads_all = HEADS
    full_width = col_width * col_count
    head_size = full_width // heads_all
    unit_count = seq_count * heads_all
    capacity = (unit_count + col_count - 1) // col_count
    pos_block = seq_len // col_count
    input_cols, gain_one, shift_one, gain_two, shift_two = (
        lax.all_gather(layer_input, "col", axis=0, tiled=True),
        lax.all_gather(first_gain, "col", axis=0, tiled=True),
        lax.all_gather(first_shift, "col", axis=0, tiled=True),
        lax.all_gather(second_gain, "col", axis=0, tiled=True),
        lax.all_gather(second_shift, "col", axis=0, tiled=True),
    )
    input_full = input_cols.T
    gain_one = gain_one.astype(jnp.float32)
    shift_one = shift_one.astype(jnp.float32)
    gain_two = gain_two.astype(jnp.float32)
    shift_two = shift_two.astype(jnp.float32)
    qkv_rows, wo_rows, up_rows, down_rows = (
        lax.all_gather(qkv_weight, "row", axis=0, tiled=True),
        lax.all_gather(out_weight, "row", axis=0, tiled=True),
        lax.all_gather(up_weight, "row", axis=0, tiled=True),
        lax.all_gather(down_weight, "row", axis=1, tiled=True),
    )
    normed_one, standard_one, inv_std_one = norm_rows(
        input_full.astype(jnp.float32), gain_one, shift_one
    )
    normed_one_low = normed_one.astype(jnp.bfloat16)
    qvb = qv_bias.astype(jnp.float32)
    bias_three = jnp.stack([qvb[0], jnp.zeros_like(qvb[0]), qvb[1]])
    qkv_local = (
        jnp.einsum("td,dje->tje", normed_one_low, qkv_rows, preferred_element_type=jnp.float32)
        + bias_three
    )
    qkv_local = qkv_local.astype(jnp.bfloat16).reshape(seq_count, seq_len, 3, col_width)
    by_position = lax.all_to_all(qkv_local, "col", split_axis=1, concat_axis=3, tiled=True)
    unit_data = by_position.reshape(seq_count, pos_block, 3, heads_all, head_size)
    unit_data = unit_data.transpose(0, 3, 1, 2, 4).reshape(unit_count, pos_block, 3, head_size)
    unit_ids = jnp.arange(unit_count)
    owners = unit_ids % col_count
    slot_rank = unit_ids // col_count
    flat_slot = owners * capacity + slot_rank
    slot_ids = jnp.arange(col_count * capacity)
    slot_owner = slot_ids // capacity
    slot_pos = slot_ids % capacity
    holder_raw = slot_pos * col_count + slot_owner
    filled = holder_raw < unit_count
    holder = jnp.where(filled, holder_raw, 0)
    send_units = jnp.take(unit_data, holder, axis=0)
    send_units = jnp.where(filled[:, None, None, None], send_units, jnp.zeros_like(send_units))
    send_units = send_units.reshape(col_count, capacity, pos_block, 3, head_size)
    received = lax.all_to_all(send_units, "col", split_axis=0, concat_axis=2, tiled=True).reshape(
        capacity, seq_len, 3, head_size
    )
    my_units = lax.dynamic_slice_in_dim(holder, column * capacity, capacity)
    my_seq = my_units // heads_all
    my_segs = jnp.take(segments, my_seq, axis=0)
    slot_outs, slot_lse = lax.map(slot_forward, (received, my_segs))
    all_outs = jax.tree.map(
        lambda part, own: part.astype(own.dtype),
        lax.all_gather(for_sending(slot_outs), "col", axis=0, tiled=True),
        slot_outs,
    )
    attn = jnp.take(all_outs, flat_slot, axis=0).reshape(seq_count, heads_all, seq_len, head_size)
    wo_heads = wo_rows.reshape(heads_all, head_size, col_width)
    projected = jnp.einsum("shtd,hde->ste", attn, wo_heads, preferred_element_type=jnp.float32)
    resid_local = (
        layer_input.astype(jnp.float32).T
        + projected.reshape(tok_rows, col_width)
        + out_bias.astype(jnp.float32)
    )
    cot_local = cotangent.astype(jnp.float32).T
    resid_cols, cot_cols = (
        lax.all_gather(resid_local.T, "col", axis=0, tiled=True),
        lax.all_gather(cot_local.T, "col", axis=0, tiled=True),
    )
    resid_full = resid_cols.T
    cot_low = cot_cols.T.astype(jnp.bfloat16)
    normed_two, standard_two, inv_std_two = norm_rows(resid_full, gain_two, shift_two)
    normed_two_low = normed_two.astype(jnp.bfloat16)
    hidden = jnp.dot(normed_two_low, up_rows, preferred_element_type=jnp.float32) + up_bias.astype(
        jnp.float32
    )
    active_low = jax.nn.gelu(hidden, approximate=True).astype(jnp.bfloat16)
    down_part = jnp.dot(active_low, down_rows, preferred_element_type=jnp.float32)
    down_local = lax.psum_scatter(
        down_part.astype(jnp.bfloat16), "col", scatter_dimension=1, tiled=True
    ).astype(jnp.float32)
    layer_output = resid_local + down_local + down_bias.astype(jnp.float32)
    grad_down = jnp.einsum("tf,td->fd", active_low, cot_low, preferred_element_type=jnp.float32)
    downbias_grad = jnp.sum(cot_local, 0)
    grad_active = jnp.einsum("td,fd->tf", cot_low, down_rows, preferred_element_type=jnp.float32)
    ignored, gelu_back = jax.vjp(lambda pre_act: jax.nn.gelu(pre_act, approximate=True), hidden)
    grad_hidden_low = gelu_back(grad_active)[0].astype(jnp.bfloat16)
    grad_up = jnp.einsum(
        "td,tf->df", normed_two_low, grad_hidden_low, preferred_element_type=jnp.float32
    )
    upbias_grad = jnp.sum(grad_hidden_low.astype(jnp.float32), 0)
    part_two = jnp.einsum("tf,df->td", grad_hidden_low, up_rows, preferred_element_type=jnp.float32)
    norm_two_part, dnorm_two, standard_two_mine = norm_back(
        part_two, standard_two, gain_two, inv_std_two, column, col_width
    )
    resid_grad = cot_local + norm_two_part
    secondgain_grad = jnp.sum(dnorm_two * standard_two_mine, 0)
    secondshift_grad = jnp.sum(dnorm_two, 0)
    proj_low = resid_grad.astype(jnp.bfloat16)
    proj_seq = proj_low.reshape(seq_count, seq_len, col_width)
    grad_out = jnp.einsum(
        "shtd,ste->hde", attn, proj_seq, preferred_element_type=jnp.float32
    ).reshape(full_width, col_width)
    outbias_grad = jnp.sum(proj_low.astype(jnp.float32), 0)
    grad_rows = jnp.take(proj_seq, holder // heads_all, axis=0)
    weight_rows = jnp.take(wo_heads, holder % heads_all, axis=0)
    terms = jnp.einsum("jte,jde->jtd", grad_rows, weight_rows, preferred_element_type=jnp.float32)
    slot_grad = lax.psum_scatter(
        jnp.where(filled[:, None, None], terms, 0.0), "col", scatter_dimension=0, tiled=True
    )
    slot_grad_low = slot_grad.astype(jnp.bfloat16)
    slot_dqkv = lax.map(slot_backward, (received, my_segs, slot_lse, slot_grad_low)).astype(
        jnp.bfloat16
    )
    back_send = slot_dqkv.reshape(capacity, col_count, pos_block, 3, head_size)
    back_recv = lax.all_to_all(back_send, "col", split_axis=1, concat_axis=0, tiled=True).reshape(
        col_count * capacity, pos_block, 3, head_size
    )
    unit_grads = jnp.take(back_recv, flat_slot, axis=0).reshape(
        seq_count, heads_all, pos_block, 3, head_size
    )
    unit_grads = unit_grads.transpose(0, 2, 3, 1, 4).reshape(seq_count, pos_block, 3, full_width)
    dqkv_local = lax.all_to_all(unit_grads, "col", split_axis=3, concat_axis=1, tiled=True).reshape(
        tok_rows, 3, col_width
    )
    grad_qkv = jnp.einsum(
        "td,tje->dje", normed_one_low, dqkv_local, preferred_element_type=jnp.float32
    )
    dqkv_sums = jnp.sum(dqkv_local.astype(jnp.float32), 0)
    qvbias_grad = jnp.stack([dqkv_sums[0], dqkv_sums[2]])
    part_one = jnp.einsum("tje,dje->td", dqkv_local, qkv_rows, preferred_element_type=jnp.float32)
    norm_one_part, dnorm_one, standard_one_mine = norm_back(
        part_one, standard_one, gain_one, inv_std_one, column, col_width
    )
    input_grad = resid_grad + norm_one_part
    firstgain_grad = jnp.sum(dnorm_one * standard_one_mine, 0)
    firstshift_grad = jnp.sum(dnorm_one, 0)
    qkv_grad, out_grad, up_grad, down_grad = (
        lax.psum_scatter(
            grad_qkv.astype(jnp.bfloat16), "row", scatter_dimension=0, tiled=True
        ).astype(jnp.float32),
        lax.psum_scatter(
            grad_out.astype(jnp.bfloat16), "row", scatter_dimension=0, tiled=True
        ).astype(jnp.float32),
        lax.psum_scatter(
            grad_up.astype(jnp.bfloat16), "row", scatter_dimension=0, tiled=True
        ).astype(jnp.float32),
        lax.psum_scatter(
            grad_down.astype(jnp.bfloat16), "row", scatter_dimension=1, tiled=True
        ).astype(jnp.float32),
    )
    (
        qvbias_grad,
        outbias_grad,
        upbias_grad,
        downbias_grad,
        firstgain_grad,
        firstshift_grad,
        secondgain_grad,
        secondshift_grad,
    ) = lax.psum(
        (
            qvbias_grad,
            outbias_grad,
            upbias_grad,
            downbias_grad,
            firstgain_grad,
            firstshift_grad,
            secondgain_grad,
            secondshift_grad,
        ),
        "row",
    )
    return (
        layer_output.T,
        input_grad.T,
        qkv_grad,
        qvbias_grad,
        out_grad,
        outbias_grad,
        up_grad,
        upbias_grad,
        down_grad,
        downbias_grad,
        firstgain_grad,
        firstshift_grad,
        secondgain_grad,
        secondshift_grad,
    )


def solution(mesh):
    placed = (
        P("col", "row"),
        P("col", "row"),
        P("row", None),
        P("row", None, "col"),
        P(None, "col"),
        P("row", "col"),
        P("col"),
        P("row", "col"),
        P("col"),
        P("col", "row"),
        P("col"),
        P("col"),
        P("col"),
        P("col"),
        P("col"),
    )
    return jax.shard_map(
        shards,
        mesh=mesh,
        in_specs=placed,
        out_specs=(
            P("col", "row"),
            P("col", "row"),
            P("row", None, "col"),
            P(None, "col"),
            P("row", "col"),
            P("col"),
            P("row", "col"),
            P("col"),
            P("col", "row"),
            P("col"),
            P("col"),
            P("col"),
            P("col"),
            P("col"),
        ),
        check_vma=False,
    )
```

profile of v0, /device:TPU:0, one launch (start us, length us, event | category | flops | bytes accessed | tf_op | source)
XLA Modules:
  0.0 1516.0 jit_solution(9843919559526337534)
XLA Ops:
  13.4 129.2 %all-reduce.17 = (bf16[1088]{0:T(1024)(128)(2,1)S(1)}, bf16[1088]{0:T(1024)(128)(2,1)S(1)}, bf16[1088]{0:T(1024)(128)(2,1)}, bf16[1088]{0:T(1024)(128)(2,1)}) all-reduce(bf16[1088]{0:T(1024)(128)(2,1)S(1)} %dynamic-update-slice.1, bf16[1088]{0:T(1024)(128)(2,1)S(1)} %dynamic-update-slice, ...), channel_id=1, replica_groups=mesh['row'=4,'col'=32] {'col'}, use_global_device_ids=true, to_apply=%add.1 | all-reduce | flops 4352 | bytes 17408
  144.3 16.2 %all_gather.39 = bf16[1088,3,34]{2,1,0:T(4,128)(2,1)S(1)} all-gather(bf16[272,3,34]{2,1,0:T(4,128)(2,1)S(1)} %copy.117), channel_id=1, replica_groups=mesh['row'=4,'col'=32] {'row'}, dimensions={0}, use_global_device_ids=true | all-gather | bytes 277440 | tf_op jit(solution)/shard_map/all_gather | solution.py:166
  161.8 5.6 convert_reduce_fusion.1
  167.5 11.9 reshape.528
  179.4 7.9 multiply_reduce_fusion.3
  187.3 7.3 subtract_multiply_fusion.1
  194.6 6.1 copy-done.2
  204.2 4.7 copy.119
  208.9 8.1 reshape.560
  217.1 4.8 all-to-all-start
  222.7 13.6 all-to-all-done
  236.2 10.7 reshape.561
  250.6 10.0 reshape.446
  269.1 4.2 all-to-all-start.1
  274.3 17.3 %all-to-all-done.1 = bf16[32,2,9216]{2,1,0:T(2,128)(2,1)S(1)} async-done(((bf16[32,2,9216]{2,1,0:T(2,128)(2,1)}), bf16[32,2,9216]{2,1,0:T(2,128)(2,1)S(1)}, u32[]{:S(2)}, u32[]{:S(2)}) %all-to-all-start.1) | async-done | bytes 1179680 | tf_op jit(solution)/shard_map/all_to_all | solution.py:198
  294.9 17.3 %while.22 = (s32[]{:T(128)}, bf16[3,1024,64]{1,2,0:T(8,128)(2,1)}, f32[3,1024]{1,0:T(4,128)}, s32[3,1024]{1,0:T(4,128)S(1)}, bf16[3,1024,3,64]{1,3,2,0:T(8,128)(2,1)S(1)}, /*index=5*/s32[]{:T(128)}, s32[]{:T(128)}, s32[]{}) while((s32[]{:T(128)}, bf16[3,1024,64]{1,2,0:T(8,128)(2,1)}, f32[3,1024]{1,0:T(4,128)}, s32[3,1024]{1,0:T(4,128)S(1)}, ...), condition=%wide.region_7.8_spmd, body=%wide.region_2.7_spmd.sunk | while | flops 280297984 | bytes 14499969 | solution.py:204
  313.0 12.0 all-gather.1
  325.5 47.4 %all-gather.11.cloned.1.call-done = bf16[96,1024,64]{1,2,0:T(8,128)(2,1)} async-done(((bf16[3,1024,64]{1,2,0:T(8,128)(2,1)}), bf16[96,1024,64]{1,2,0:T(8,128)(2,1)}) %all-gather.11.cloned.1.call-update) | async-done | bytes 12582928 | tf_op jit(solution)/shard_map/all_gather | solution.py:207
  372.8 10.3 gather_fusion.2
  383.1 8.2 fusion.128
  391.4 8.6 copy.159
  400.0 5.2 fusion.105
  407.3 13.1 all-gather.3
  420.8 13.0 all-gather.4
  435.9 10.6 reshape.529
  446.5 6.6 fusion.106
  453.1 63.9 %all-gather.15.cloned.1.call-done = f32[32,34,4096]{2,1,0:T(8,128)} async-done(((f32[1,34,4096]{2,1,0:T(8,128)}), f32[32,34,4096]{2,1,0:T(8,128)}) %all-gather.15.cloned.1.call-update) | async-done | bytes 17825808 | tf_op jit(solution)/shard_map/all_gather | solution.py:220
  516.9 8.0 reduce_sum.182
  524.9 15.3 %reshape.521 = f32[1088,4096]{1,0:T(8,128)} reshape(f32[32,34,4096]{2,1,0:T(8,128)} %all-gather.15.cloned.1.call-done) | data formatting | bytes 35651584
  540.2 7.9 multiply_reduce_fusion.2
  548.1 13.8 fusion.26
  561.9 5.0 convert_reduce_fusion.2
  566.9 11.3 multiply_reduce_fusion.5
  580.0 125.2 %fusion.1 = f32[4096,40]{0,1:T(8,128)S(1)} fusion(f32[4096,1088]{0,1:T(8,128)} %get-tuple-element.214), kind=kCustom, calls=%all-reduce-scatter.1 | all-reduce-scatter fusion | flops 5242881 | bytes 18481664
  713.0 5.3 collective-permute-start.5
  720.4 97.3 %all-reduce.23.cloned.1.call-done = (f32[4096,32]{0,1:T(8,128)}, f32[4096,32]{0,1:T(8,128)}) async-done(((f32[4096,32]{0,1:T(8,128)}, f32[4096,32]{0,1:T(8,128)}), (f32[4096,32]{0,1:T(8,128)}, f32[4096,32]{0,1:T(8,128)})) %all-reduce.23.cloned.1.call-update) | async-done | bytes 1048592
  820.9 18.4 %concatenate.22 = f32[4096,226]{0,1:T(8,128)} concatenate(f32[4096,26]{0,1:T(8,128)} %collective-permute-done.9, f32[4096,40]{0,1:T(8,128)} %collective-permute-done.8, f32[4096,40]{0,1:T(8,128)} %collective-permute-done.7, f32[4096,40]{0,1:T(8,128)} %collective-permute-done.6, f32[4096,40]{0,1:T(8,128)} %collective-permute-done.5, f32[4096,40]{0,1:T(8,128)S(1)} %fusion.1), dimensions={1} | concatenate | bytes 7405568
  842.0 6.7 gather_fusion.3
  848.7 14.3 broadcast_select_fusion
  864.1 7.7 convolution_convert_fusion.2
  871.7 131.3 %fusion = bf16[4096,40]{0,1:T(8,128)(2,1)} fusion(bf16[4096,1088]{0,1:T(8,128)(2,1)} %convolution_convert_fusion.2), kind=kCustom, calls=%all-reduce-scatter | all-reduce-scatter fusion | flops 5242881 | bytes 9241088
  1013.0 6.7 convolution_convert_fusion.4
  1020.8 7.2 convolution_convert_fusion.3
  1030.4 11.1 reduce-scatter.20.cloned.1.call-done
  1042.7 22.1 %while.23 = (s32[]{:T(128)}, bf16[3,1024,3,64]{1,3,2,0:T(8,128)(2,1)S(1)}, s32[3,1024]{1,0:T(4,128)S(1)}, bf16[3,1024,3,64]{1,3,2,0:T(8,128)(2,1)}, f32[3,1024]{...) while((s32[]{:T(128)}, bf16[3,1024,3,64]{1,3,2,0:T(8,128)(2,1)S(1)}, ...), condition=%wide.region_20.21_spmd, body=%wide.region_17.20_spmd.sunk | while | flops 685571584 | bytes 36098212 | solution.py:265
  1070.5 5.0 reshape.564
  1075.4 6.4 all-to-all-start.2
  1082.3 8.0 broadcast_select_fusion.1
  1090.3 16.9 %concatenate.21 = bf16[4096,226]{0,1:T(8,128)(2,1)} concatenate(bf16[4096,26]{0,1:T(8,128)(2,1)S(1)} %collective-permute-done.4, bf16[4096,40]{0,1:T(8,128)(2,1)} %collective-permute-done.3, bf16[4096,40]{0,1:T(8,128)(2,1)} %collective-permute-done.2, bf16[4096,40]{0,1:T(8,128)(2,1)} %collective-permute-done.1, bf16[4096,40]{0,1:T(8,128)(2,1)} %collective-permute-done, ...), dimensions={1} | concatenate | bytes 3702784
  1107.2 6.3 fusion.37
  1121.6 7.8 copy.144
  1129.5 4.0 reshape.566
  1133.4 7.5 all-to-all-start.3
  1148.6 6.7 all-to-all-done.3
  1155.3 5.5 reshape.567
  1163.5 5.8 reshape.454
  1169.3 10.3 convolution_convert_fusion.5
  1179.6 11.2 multiply_reduce_fusion.4
  1194.4 123.0 %fusion.2 = f32[4096,40]{0,1:T(8,128)} fusion(f32[4096,1088]{0,1:T(8,128)} %get-tuple-element.215), kind=kCustom, calls=%all-reduce-scatter.2 | all-reduce-scatter fusion | flops 5242881 | bytes 18481664
  1317.4 7.3 copy.145
  1333.1 5.3 collective-permute-start.10
  1345.0 127.4 %all-reduce.21.cloned.1.call-done = (f32[4096,32]{0,1:T(8,128)}, f32[4096,32]{0,1:T(8,128)}) async-done(((f32[4096,32]{0,1:T(8,128)}, f32[4096,32]{0,1:T(8,128)}), (f32[4096,32]{0,1:T(8,128)}, f32[4096,32]{0,1:T(8,128)})) %all-reduce.21.cloned.1.call-update) | async-done | bytes 1048592
  1475.6 18.7 %concatenate.23 = f32[4096,226]{0,1:T(8,128)} concatenate(f32[4096,26]{0,1:T(8,128)} %collective-permute-done.14, f32[4096,40]{0,1:T(8,128)} %collective-permute-done.13, f32[4096,40]{0,1:T(8,128)} %collective-permute-done.12, f32[4096,40]{0,1:T(8,128)} %collective-permute-done.11, f32[4096,40]{0,1:T(8,128)} %collective-permute-done.10, f32[4096,40]{0,1:T(8,128)} %fusion.2), dimensions={1} | concatenate | bytes 7405568
  1497.9 11.3 all-reduce.16
  (371 shorter events, 156.0 us)
Async XLA Ops:
  7.2 266.5 %copy-start = (s32[4,1024]{1,0:T(4,128)S(1)}, s32[4,1024]{1,0:T(4,128)}, u32[]{:S(2)}) copy-start(s32[4,1024]{1,0:T(4,128)} %param.21) | copy-start | bytes 49156
  7.2 154.5 %copy-start.44 = (bf16[2,34]{1,0:T(2,128)(2,1)S(1)}, bf16[2,34]{1,0:T(2,128)(2,1)}, u32[]{:S(2)}) copy-start(bf16[2,34]{1,0:T(2,128)(2,1)} %param.23) | copy-start | bytes 412
  7.2 154.6 %all-gather.13.cloned.1.call-start = ((), (), s32[]{:S(2)}) async-start(), calls=%async_computation.11 | async-start | bytes 10813440 | tf_op jit(solution)/shard_map/all_gather | solution.py:154
  142.5 52.0 %copy-start.31 = (f32[1088]{0:T(1024)}, f32[1088]{0:T(1024)S(1)}, u32[]{:S(2)}) copy-start(f32[1088]{0:T(1024)S(1)} %convert_element_type.130) | copy-start | bytes 13060
  143.1 51.4 %copy-start.34 = (f32[1088]{0:T(1024)}, f32[1088]{0:T(1024)S(1)}, u32[]{:S(2)}) copy-start(f32[1088]{0:T(1024)S(1)} %convert_element_type.131) | copy-start | bytes 13060
  161.7 32.9 %copy-start.17 = (bf16[1088,3,34]{0,2,1:T(8,128)(2,1)}, bf16[1088,3,34]{0,2,1:T(8,128)(2,1)S(1)}, u32[]{:S(2)}) copy-start(bf16[1088,3,34]{0,2,1:T(8,128)(2,1)S(1)} %copy.118) | copy-start | bytes 665860
  217.1 19.2 %all-to-all-start = ((bf16[32,2,6528]{2,1,0:T(2,128)(2,1)}), bf16[32,2,6528]{2,1,0:T(2,128)(2,1)}, u32[]{:S(2)}, u32[]{:S(2)}) async-start(bf16[32,2,6528]{2,1,0:T(2,128)(2,1)} %reshape.560), calls=%async_computation | async-start | bytes 1671168 | tf_op jit(solution)/shard_map/all_to_all | solution.py:182
  269.1 22.5 %all-to-all-start.1 = ((bf16[32,2,9216]{2,1,0:T(2,128)(2,1)}), bf16[32,2,9216]{2,1,0:T(2,128)(2,1)S(1)}, u32[]{:S(2)}, u32[]{:S(2)}) async-start(bf16[32,2,9216]{2,1,0:T(2,128)(2,1)} %reshape.562), calls=%async_computation.1 | async-start | bytes 2359296 | tf_op jit(solution)/shard_map/all_to_all | solution.py:198
  273.3 99.6 %all-gather.11.cloned.1.call-start = ((), (), s32[]{:S(2)}) async-start(), calls=%async_computation.9 | async-start | bytes 12976128 | tf_op jit(solution)/shard_map/all_gather | solution.py:207
  294.9 18.1 %copy-start.50 = (bf16[34]{0:T(256)(128)(2,1)S(1)}, bf16[34]{0:T(256)(128)(2,1)}, u32[]{:S(2)}) copy-start(bf16[34]{0:T(256)(128)(2,1)} %param.25) | copy-start | bytes 208
  294.9 18.1 %copy-start.33 = (bf16[272,34]{0,1:T(8,128)(2,1)S(1)}, bf16[272,34]{0,1:T(8,128)(2,1)}, u32[]{:S(2)}) copy-start(bf16[272,34]{0,1:T(8,128)(2,1)} %param.24) | copy-start | bytes 55492
  312.2 70.9 %copy-start.3 = (bf16[3,1024,3,64]{1,3,2,0:T(8,128)(2,1)}, bf16[3,1024,3,64]{1,3,2,0:T(8,128)(2,1)S(1)}, u32[]{:S(2)}) copy-start(bf16[3,1024,3,64]{1,3,2,0:T(8,128)(2,1)S(1)} %get-tuple-element.393) | copy-start | bytes 3538948
  312.2 70.9 %copy-start.19 = (s32[3,1024]{1,0:T(4,128)}, s32[3,1024]{1,0:T(4,128)S(1)}, u32[]{:S(2)}) copy-start(s32[3,1024]{1,0:T(4,128)S(1)} %get-tuple-element.432) | copy-start | bytes 36868
  312.2 123.7 %all-gather.17.cloned.1.call-start = ((), (), s32[]{:S(2)}) async-start(), calls=%async_computation.13 | async-start | bytes 10813440 | tf_op jit(solution)/shard_map/all_gather | solution.py:221
  313.0 204.0 %all-gather.15.cloned.1.call-start = ((), (), s32[]{:S(2)}) async-start(), calls=%async_computation.12 | async-start | bytes 21626880 | tf_op jit(solution)/shard_map/all_gather | solution.py:220
  313.0 92.2 %copy-start.42 = (f32[34]{0:T(128)}, f32[34]{0:T(128)S(1)}, u32[]{:S(2)}) copy-start(f32[34]{0:T(128)S(1)} %convert_element_type.135) | copy-start | bytes 412
  325.4 57.7 %copy-start.37 = (pred[4,17]{1,0:T(4,128)(4,1)}, pred[4,17]{1,0:T(4,128)(4,1)S(1)}, u32[]{:S(2)}) copy-start(pred[4,17]{1,0:T(4,128)(4,1)S(1)} %compare_and_fusion.4) | copy-start | bytes 208
  325.4 57.7 %copy-start.36 = (s32[1024]{0:T(1024)}, s32[1024]{0:T(1024)S(1)}, u32[]{:S(2)}) copy-start(s32[1024]{0:T(1024)S(1)} %pad_clamp_fusion.2) | copy-start | bytes 12292
  406.1 14.7 copy-start.30
  407.1 410.6 %all-reduce.23.cloned.1.call-start = ((), (), s32[]{:S(2)}) async-start(), calls=%async_computation.19 | async-start | bytes 2097152
  407.3 432.1 %copy-start.45 = (f32[34]{0:T(128)}, f32[34]{0:T(128)S(1)}, u32[]{:S(2)}) copy-start(f32[34]{0:T(128)S(1)} %dynamic_slice.38) | copy-start | bytes 412
  434.3 12.2 copy-start.14
  548.1 291.2 %copy-start.21 = (f32[4096]{0:T(1024)}, f32[4096]{0:T(1024)S(1)}, u32[]{:S(2)}) copy-start(f32[4096]{0:T(1024)S(1)} %add_rsqrt_fusion) | copy-start | bytes 49156
  548.1 13.8 copy-start.10
  580.0 461.5 %reduce-scatter.20.cloned.1.call-start = ((), (), s32[]{:S(2)}) async-start(), calls=%async_computation.10 | async-start | bytes 25952256 | tf_op jit(solution)/shard_map/reduce_scatter | solution.py:261
  706.1 114.9 %collective-permute-start.8 = (f32[4096,40]{0,1:T(8,128)S(1)}, f32[4096,40]{0,1:T(8,128)}, u32[]{:S(2)}, u32[]{:S(2)}) collective-permute-start(f32[4096,40]{0,1:T(8,128)S(1)} %fusion.1), channel_id=1, source_target_pairs={{0,4},{1,5},{2,6},{3,7},{4,8},{5,9},{6,10},{7,11},{8,12},{9,13},{1... | collective-permute-start | bytes 1966088
  708.2 112.7 %collective-permute-start.7 = (f32[4096,40]{0,1:T(8,128)S(1)}, f32[4096,40]{0,1:T(8,128)}, u32[]{:S(2)}, u32[]{:S(2)}) collective-permute-start(f32[4096,40]{0,1:T(8,128)S(1)} %fusion.1), channel_id=1, source_target_pairs={{0,3},{1,4},{2,5},{3,6},{4,7},{5,8},{6,9},{7,10},{8,11},{9,12},{10... | collective-permute-start | bytes 1966088
  710.3 110.6 %collective-permute-start.6 = (f32[4096,40]{0,1:T(8,128)S(1)}, f32[4096,40]{0,1:T(8,128)}, u32[]{:S(2)}, u32[]{:S(2)}) collective-permute-start(f32[4096,40]{0,1:T(8,128)S(1)} %fusion.1), channel_id=1, source_target_pairs={{0,2},{1,3},{2,4},{3,5},{4,6},{5,7},{6,8},{7,9},{8,10},{9,11},{10,... | collective-permute-start | bytes 1966088
  713.0 107.9 %collective-permute-start.5 = (f32[4096,40]{0,1:T(8,128)S(1)}, f32[4096,40]{0,1:T(8,128)}, u32[]{:S(2)}, u32[]{:S(2)}) collective-permute-start(f32[4096,40]{0,1:T(8,128)S(1)} %fusion.1), channel_id=1, source_target_pairs={{0,1},{1,2},{2,3},{3,4},{4,5},{5,6},{6,7},{7,8},{8,9},{9,10},{10,1... | collective-permute-start | bytes 1966088
  718.3 102.6 %collective-permute-start.9 = (f32[4096,26]{0,1:T(8,128)}, f32[4096,26]{0,1:T(8,128)}, u32[]{:S(2)}, u32[]{:S(2)}) collective-permute-start(f32[4096,26]{0,1:T(8,128)} %slice.115), channel_id=1, source_target_pairs={{0,5},{1,6},{2,7},{3,8},{4,9},{5,10},{6,11},{7,12},{8,13},{9,14},{... | collective-permute-start | bytes 1277960
  819.3 20.1 %copy-start.25 = (f32[4096,1]{0,1:T(1,128)}, f32[4096,1]{0,1:T(1,128)S(1)}, u32[]{:S(2)}) copy-start(f32[4096,1]{0,1:T(1,128)S(1)} %constant_dynamic-slice_fusion.5) | copy-start | bytes 49156
  820.9 18.5 %copy-start.27 = (f32[4096,1]{0,1:T(1,128)}, f32[4096,1]{0,1:T(1,128)S(1)}, u32[]{:S(2)}) copy-start(f32[4096,1]{0,1:T(1,128)S(1)} %dynamic-slice_multiply_fusion.1) | copy-start | bytes 49156
  820.9 18.5 %copy-start.8 = (bf16[34,4096]{1,0:T(8,128)(2,1)S(1)}, bf16[34,4096]{1,0:T(8,128)(2,1)}, u32[]{:S(2)}) copy-start(bf16[34,4096]{1,0:T(8,128)(2,1)} %param.20) | copy-start | bytes 835588
  863.0 280.5 %reduce-scatter.26.cloned.1.call-start = ((), (), s32[]{:S(2)}) async-start(), calls=%async_computation.16 | async-start | bytes 696320
  1004.7 85.5 %collective-permute-start.3 = (bf16[4096,40]{0,1:T(8,128)(2,1)}, bf16[4096,40]{0,1:T(8,128)(2,1)}, u32[]{:S(2)}, u32[]{:S(2)}) collective-permute-start(bf16[4096,40]{0,1:T(8,128)(2,1)} %fusion), channel_id=1, source_target_pairs={{0,4},{1,5},{2,6},{3,7},{4,8},{5,9},{6,10},{7,11},{8,12},{9,13},{1... | collective-permute-start | bytes 983048
  1006.8 83.5 %collective-permute-start.2 = (bf16[4096,40]{0,1:T(8,128)(2,1)}, bf16[4096,40]{0,1:T(8,128)(2,1)}, u32[]{:S(2)}, u32[]{:S(2)}) collective-permute-start(bf16[4096,40]{0,1:T(8,128)(2,1)} %fusion), channel_id=1, source_target_pairs={{0,3},{1,4},{2,5},{3,6},{4,7},{5,8},{6,9},{7,10},{8,11},{9,12},{10... | collective-permute-start | bytes 983048
  1008.8 81.5 %collective-permute-start.1 = (bf16[4096,40]{0,1:T(8,128)(2,1)}, bf16[4096,40]{0,1:T(8,128)(2,1)}, u32[]{:S(2)}, u32[]{:S(2)}) collective-permute-start(bf16[4096,40]{0,1:T(8,128)(2,1)} %fusion), channel_id=1, source_target_pairs={{0,2},{1,3},{2,4},{3,5},{4,6},{5,7},{6,8},{7,9},{8,10},{9,11},{10,... | collective-permute-start | bytes 983048
  1010.8 79.5 %collective-permute-start = (bf16[4096,40]{0,1:T(8,128)(2,1)}, bf16[4096,40]{0,1:T(8,128)(2,1)}, u32[]{:S(2)}, u32[]{:S(2)}) collective-permute-start(bf16[4096,40]{0,1:T(8,128)(2,1)} %fusion), channel_id=1, source_target_pairs={{0,1},{1,2},{2,3},{3,4},{4,5},{5,6},{6,7},{7,8},{8,9},{9,10},{10,1... | collective-permute-start | bytes 983048
  1020.8 124.5 %reduce-scatter.28.cloned.1.call-start = ((), (), s32[]{:S(2)}) async-start(), calls=%async_computation.17 | async-start | bytes 696320
  1028.0 14.7 copy-start.20
  1029.0 61.2 %collective-permute-start.4 = (bf16[4096,26]{0,1:T(8,128)(2,1)}, bf16[4096,26]{0,1:T(8,128)(2,1)S(1)}, u32[]{:S(2)}, u32[]{:S(2)}) collective-permute-start(bf16[4096,26]{0,1:T(8,128)(2,1)} %slice.114), channel_id=1, source_target_pairs={{0,5},{1,6},{2,7},{3,8},{4,9},{5,10},{6,11},{7,12},{8,13},{9,14},{... | collective-permute-start | bytes 638984
  1070.5 11.8 copy-start.38
  1075.4 39.0 %all-to-all-start.2 = ((bf16[32,2,9216]{2,1,0:T(2,128)(2,1)}), bf16[32,2,9216]{2,1,0:T(2,128)(2,1)S(1)}, u32[]{:S(2)}, u32[]{:S(2)}) async-start(bf16[32,2,9216]{2,1,0:T(2,128)(2,1)} %reshape.564), calls=%async_computation.3 | async-start | bytes 2359296 | tf_op jit(solution)/shard_map/all_to_all | solution.py:269
  1081.8 65.1 %reduce-scatter.24.cloned.1.call-start = ((), (), s32[]{:S(2)}) async-start(), calls=%async_computation.15 | async-start | bytes 348160
  1090.3 17.0 %copy-start.13 = (bf16[4,1024,34]{1,0,2:T(4,128)(2,1)S(1)}, bf16[4,1024,34]{1,0,2:T(4,128)(2,1)}, u32[]{:S(2)}) copy-start(bf16[4,1024,34]{1,0,2:T(4,128)(2,1)} %copy-done.12) | copy-start | bytes 835588
  1129.4 11.7 copy-start.43
  1133.4 21.9 %all-to-all-start.3 = ((bf16[32,2,6528]{2,1,0:T(2,128)(2,1)}), bf16[32,2,6528]{2,1,0:T(2,128)(2,1)}, u32[]{:S(2)}, u32[]{:S(2)}) async-start(bf16[32,2,6528]{2,1,0:T(2,128)(2,1)} %reshape.566), calls=%async_computation.4 | async-start | bytes 1671168 | tf_op jit(solution)/shard_map/all_to_all | solution.py:276
  1140.9 202.1 %reduce-scatter.22.cloned.1.call-start = ((), (), s32[]{:S(2)}) async-start(), calls=%async_computation.14 | async-start | bytes 348160
  1169.3 10.3 copy-start.6
  1169.3 10.3 copy-start.18
  1194.4 278.0 %all-reduce.21.cloned.1.call-start = ((), (), s32[]{:S(2)}) async-start(), calls=%async_computation.18 | async-start | bytes 2097152
  1324.7 17.7 %copy-start.4 = (bf16[4,32,3,32,34]{4,3,1,2,0:T(8,128)(2,1)S(1)}, bf16[4,32,3,32,34]{4,3,1,2,0:T(8,128)(2,1)}, u32[]{:S(2)}) copy-start(bf16[4,32,3,32,34]{4,3,1,2,0:T(8,128)(2,1)} %copy.145) | copy-start | bytes 2506756
  1326.7 148.9 %collective-permute-start.13 = (f32[4096,40]{0,1:T(8,128)}, f32[4096,40]{0,1:T(8,128)}, u32[]{:S(2)}, u32[]{:S(2)}) collective-permute-start(f32[4096,40]{0,1:T(8,128)} %fusion.2), channel_id=1, source_target_pairs={{0,4},{1,5},{2,6},{3,7},{4,8},{5,9},{6,10},{7,11},{8,12},{9,13},{1... | collective-permute-start | bytes 1966088
  1328.8 146.8 %collective-permute-start.12 = (f32[4096,40]{0,1:T(8,128)}, f32[4096,40]{0,1:T(8,128)}, u32[]{:S(2)}, u32[]{:S(2)}) collective-permute-start(f32[4096,40]{0,1:T(8,128)} %fusion.2), channel_id=1, source_target_pairs={{0,3},{1,4},{2,5},{3,6},{4,7},{5,8},{6,9},{7,10},{8,11},{9,12},{10... | collective-permute-start | bytes 1966088
  1330.9 144.6 %collective-permute-start.11 = (f32[4096,40]{0,1:T(8,128)}, f32[4096,40]{0,1:T(8,128)}, u32[]{:S(2)}, u32[]{:S(2)}) collective-permute-start(f32[4096,40]{0,1:T(8,128)} %fusion.2), channel_id=1, source_target_pairs={{0,2},{1,3},{2,4},{3,5},{4,6},{5,7},{6,8},{7,9},{8,10},{9,11},{10,... | collective-permute-start | bytes 1966088
  1333.1 142.5 %collective-permute-start.10 = (f32[4096,40]{0,1:T(8,128)}, f32[4096,40]{0,1:T(8,128)}, u32[]{:S(2)}, u32[]{:S(2)}) collective-permute-start(f32[4096,40]{0,1:T(8,128)} %fusion.2), channel_id=1, source_target_pairs={{0,1},{1,2},{2,3},{3,4},{4,5},{5,6},{6,7},{7,8},{8,9},{9,10},{10,1... | collective-permute-start | bytes 1966088
  1338.3 137.2 %collective-permute-start.14 = (f32[4096,26]{0,1:T(8,128)}, f32[4096,26]{0,1:T(8,128)}, u32[]{:S(2)}, u32[]{:S(2)}) collective-permute-start(f32[4096,26]{0,1:T(8,128)} %slice.116), channel_id=1, source_target_pairs={{0,5},{1,6},{2,7},{3,8},{4,9},{5,10},{6,11},{7,12},{8,13},{9,14},{... | collective-permute-start | bytes 1277960
  1475.5 18.8 %copy-start.9 = (bf16[34,4096]{1,0:T(8,128)(2,1)S(1)}, bf16[34,4096]{1,0:T(8,128)(2,1)}, u32[]{:S(2)}) copy-start(bf16[34,4096]{1,0:T(8,128)(2,1)} %param.20) | copy-start | bytes 835588
  1475.5 18.8 %copy-start.22 = (f32[4096]{0:T(1024)S(1)}, f32[4096]{0:T(1024)}, u32[]{:S(2)}) copy-start(f32[4096]{0:T(1024)} %copy-done.21) | copy-start | bytes 49156
  1475.5 18.8 %copy-start.24 = (f32[4096]{0:T(1024)S(1)}, f32[4096]{0:T(1024)}, u32[]{:S(2)}) copy-start(f32[4096]{0:T(1024)} %copy-done.23) | copy-start | bytes 49156
  1475.5 18.8 %copy-start.26 = (f32[4096,1]{0,1:T(1,128)S(1)}, f32[4096,1]{0,1:T(1,128)}, u32[]{:S(2)}) copy-start(f32[4096,1]{0,1:T(1,128)} %copy-done.25) | copy-start | bytes 49156
  1475.5 18.8 %copy-start.28 = (f32[4096,1]{0,1:T(1,128)S(1)}, f32[4096,1]{0,1:T(1,128)}, u32[]{:S(2)}) copy-start(f32[4096,1]{0,1:T(1,128)} %copy-done.27) | copy-start | bytes 49156
  1475.5 18.8 %copy-start.46 = (f32[34]{0:T(128)S(1)}, f32[34]{0:T(128)}, u32[]{:S(2)}) copy-start(f32[34]{0:T(128)} %copy-done.45) | copy-start | bytes 412
  1475.6 33.6 %copy-start.1 = (s32[4,1024]{1,0:T(4,128)S(1)}, s32[4,1024]{1,0:T(4,128)}, u32[]{:S(2)}) copy-start(s32[4,1024]{1,0:T(4,128)} %param.21) | copy-start | bytes 49156
  (19 other events, 61.0 us)
Sparse Core Ops, SparseCore 0:
  10.3 60.4 all-gather.12
  312.3 60.4 all-gather.10
  375.1 57.2 all-gather.16
  435.1 81.7 all-gather.14
  580.1 237.5 all-reduce.22
  863.2 178.2 reduce-scatter.19
  1043.9 22.2 reduce-scatter.25
  1068.7 21.3 reduce-scatter.27
  1114.6 22.4 reduce-scatter.23
  1194.5 19.2 reduce-scatter.21
  1342.5 129.8 all-reduce.20
where the time goes:
time: 1530 us; the launch traced here: 1520 us
  blocking collectives  574 us (38%)
  waiting for transfers between devices  386 us (25%)
  local copies, waits for them, and re-layouts  265 us (17%)
  matrix products  116 us (8%)
  other arithmetic  95.6 us (6%)
  starting transfers between devices  61.9 us (4%)
  between operations  16.6 us (1%)
    unnamed x4, blocking collectives  509 us
    unnamed x32, waiting for transfers between devices  226 us
    unnamed x145, local copies, waits for them, and re-layouts  142 us
    all_gather x1, waiting for transfers between devices, shards(): lax.all_gather(resid_local.T, 'col', axis=0, tiled=True)  63.9 us
    all_gather x1, waiting for transfers between devices, shards(): lax.all_gather(for_sending(slot_outs), 'col', axis=0, tiled=True)  47.4 us
    unnamed x21, starting transfers between devices  38.6 us
  transfers between devices with their start and end apart: 30, of which 8 were waited for; matrix products, arithmetic and copies ran while one was open for 38% of the time, Pallas kernels for 0%

commit v1 on v0

v1 whole, which is shorter than its diff:
```python
import functools

import jax
import jax.numpy as jnp
from jax import lax
from jax.experimental import pallas as pl
from jax.experimental.pallas import tpu as pltpu
from jax.sharding import Mesh, PartitionSpec as P

HEADS = 17
HD = 64
EPS = 1e-05
XY = ("x", "y")
COL = ("x", "y", "core")
F32 = jnp.float32
BF16 = jnp.bfloat16
QB = 256


def nn(a, b):
    return lax.dot_general(a, b, (((1,), (0,)), ((), ())), preferred_element_type=F32)


def nt(a, b):
    return lax.dot_general(a, b, (((1,), (1,)), ((), ())), preferred_element_type=F32)


def masked_scores(k, q_block, seg_col, seg_row, start, keys):
    scores = nn(k[:keys], q_block)
    key_pos = lax.broadcasted_iota(jnp.int32, scores.shape, 0)
    query_pos = lax.broadcasted_iota(jnp.int32, scores.shape, 1) + start
    allowed = (key_pos <= query_pos) & (seg_col[:keys] == seg_row[:, start : start + QB])
    return jnp.where(allowed, scores, -1e30)


def attend_kernel(count_ref, qkv_ref, seg_row_ref, seg_col_ref, out_ref, lse_ref):
    valid = pl.program_id(0) < count_ref[0]

    @pl.when(valid)
    def _():
        q = qkv_ref[0, 0] * (HD**-0.5)
        k = qkv_ref[0, 1].T
        v = qkv_ref[0, 2]
        length = q.shape[1]
        for start in range(0, length, QB):
            keys = start + QB
            scores = masked_scores(
                k, q[:, start:keys], seg_col_ref[...], seg_row_ref[...], start, keys
            )
            top = jnp.max(scores, 0, keepdims=True)
            weights = jnp.exp(scores - top)
            total = jnp.sum(weights, 0, keepdims=True)
            result = nn(v[:, :keys], weights.astype(BF16)) * (1.0 / total)
            out_ref[0, :, start:keys] = result.astype(BF16)
            lse_ref[0, :, start:keys] = top + jnp.log(total)

    @pl.when(jnp.logical_not(valid))
    def _():
        out_ref[...] = jnp.zeros_like(out_ref)
        lse_ref[...] = jnp.zeros_like(lse_ref)


def attend_back_kernel(
    count_ref, qkv_ref, seg_row_ref, seg_col_ref, out_ref, lse_ref, grad_ref, dqkv_ref, dk_ref, dv_ref
):
    valid = pl.program_id(0) < count_ref[0]

    @pl.when(valid)
    def _():
        q = qkv_ref[0, 0] * (HD**-0.5)
        key_cols = qkv_ref[0, 1]
        k = key_cols.T
        v = qkv_ref[0, 2].T
        grad = grad_ref[0]
        length = q.shape[1]
        delta = jnp.sum(grad.astype(F32) * out_ref[0].astype(F32), 0, keepdims=True)
        dk_ref[...] = jnp.zeros_like(dk_ref)
        dv_ref[...] = jnp.zeros_like(dv_ref)
        for start in range(0, length, QB):
            keys = start + QB
            scores = masked_scores(
                k, q[:, start:keys], seg_col_ref[...], seg_row_ref[...], start, keys
            )
            weights = jnp.exp(scores - lse_ref[0, :, start:keys])
            dweights = nn(v[:keys], grad[:, start:keys])
            dscores = (weights * (dweights - delta[:, start:keys])).astype(BF16)
            dq = nn(key_cols[:, :keys], dscores) * (HD**-0.5)
            dqkv_ref[0, 0, :, start:keys] = dq.astype(BF16)
            dk_ref[:, :keys] += nt(q[:, start:keys], dscores)
            dv_ref[:, :keys] += nt(grad[:, start:keys], weights.astype(BF16))
        dqkv_ref[0, 1] = dk_ref[...].astype(BF16)
        dqkv_ref[0, 2] = dv_ref[...].astype(BF16)

    @pl.when(jnp.logical_not(valid))
    def _():
        dqkv_ref[...] = jnp.zeros_like(dqkv_ref)


def slot_spec(*dims):
    return pl.BlockSpec((1,) + dims, lambda s: (s,) + (0,) * len(dims))


def whole_spec(*dims):
    return pl.BlockSpec(dims, lambda s: (0,) * len(dims))


def attend(count, qkv, seg_row, seg_col):
    slots, _, _, length = qkv.shape
    return pl.pallas_call(
        attend_kernel,
        grid=(slots,),
        in_specs=[
            pl.BlockSpec(memory_space=pltpu.SMEM),
            slot_spec(3, HD, length),
            whole_spec(1, length),
            whole_spec(length, 1),
        ],
        out_specs=[slot_spec(HD, length), slot_spec(1, length)],
        out_shape=[
            jax.ShapeDtypeStruct((slots, HD, length), BF16),
            jax.ShapeDtypeStruct((slots, 1, length), F32),
        ],
        compiler_params=pltpu.CompilerParams(vmem_limit_bytes=40 * 2**20),
    )(count, qkv, seg_row, seg_col)


def attend_back(count, qkv, seg_row, seg_col, out, lse, grad):
    slots, _, _, length = qkv.shape
    return pl.pallas_call(
        attend_back_kernel,
        grid=(slots,),
        in_specs=[
            pl.BlockSpec(memory_space=pltpu.SMEM),
            slot_spec(3, HD, length),
            whole_spec(1, length),
            whole_spec(length, 1),
            slot_spec(HD, length),
            slot_spec(1, length),
            slot_spec(HD, length),
        ],
        out_specs=slot_spec(3, HD, length),
        out_shape=jax.ShapeDtypeStruct((slots, 3, HD, length), BF16),
        scratch_shapes=[pltpu.VMEM((HD, length), F32), pltpu.VMEM((HD, length), F32)],
        compiler_params=pltpu.CompilerParams(vmem_limit_bytes=40 * 2**20),
    )(count, qkv, seg_row, seg_col, out, lse, grad)


def norm(v, gain, shift):
    centred = v - jnp.mean(v, 0, keepdims=True)
    inv_std = lax.rsqrt(jnp.mean(centred * centred, 0, keepdims=True) + EPS)
    standard = centred * inv_std
    return (standard * gain + shift).astype(BF16), standard, inv_std


def norm_back(dn, standard, inv_std, gain):
    dv = dn * gain
    back = inv_std * (
        dv - jnp.mean(dv, 0, keepdims=True) - standard * jnp.mean(dv * standard, 0, keepdims=True)
    )
    return back, jnp.sum(dn * standard, 1), jnp.sum(dn, 1)


def to_heads(v, core):
    n, _, tokens = v.shape
    heads = v.reshape(n, HEADS, HD, tokens).transpose(1, 0, 2, 3)
    pairs = heads[:16].reshape(2, 4, 2, n, HD, tokens)
    mine = lax.dynamic_index_in_dim(pairs, core, 2, keepdims=False)
    last = jnp.broadcast_to(heads[16:], (4, n, HD, tokens))
    return jnp.concatenate([mine.transpose(1, 0, 2, 3, 4), last[:, None]], 1)


def swap_heads(send):
    got = lax.all_to_all(send, "y", split_axis=0, concat_axis=0, tiled=True)
    _, slots, n, _, tokens = got.shape
    return got.transpose(1, 2, 3, 0, 4).reshape(slots, n, HD, 4 * tokens)


def from_heads(v):
    slots, n, _, length = v.shape
    send = v.reshape(slots, n, HD, 4, length // 4).transpose(3, 0, 1, 2, 4)
    send = jnp.repeat(send, 2, axis=0)
    got = lax.all_to_all(send, ("y", "core"), split_axis=0, concat_axis=0, tiled=True)
    got = got.transpose(2, 1, 0, 3, 4).reshape(n, slots * 8, HD, length // 4)
    return got[:, :HEADS].reshape(n, HEADS * HD, length // 4)


def shards(
    layer_input,
    cotangent,
    segments,
    qkv_weight,
    qv_bias,
    out_weight,
    out_bias,
    up_weight,
    up_bias,
    down_weight,
    down_bias,
    first_gain,
    first_shift,
    second_gain,
    second_shift,
):
    ix, iy, core = lax.axis_index("x"), lax.axis_index("y"), lax.axis_index("core")
    width = layer_input.shape[0]
    rows = qkv_weight.shape[0]
    full = 4 * rows
    units = up_weight.shape[1]

    small = jnp.concatenate(
        [qv_bias, jnp.stack([out_bias, first_gain, first_shift, second_gain, second_shift])], 0
    ).reshape(1, 7 * width)
    block = jnp.concatenate(
        [
            qkv_weight.transpose(1, 2, 0).reshape(3 * width, rows),
            jnp.pad(small, ((0, 0), (0, rows - 7 * width))),
            jnp.pad(up_bias[None], ((0, 0), (0, rows - units))),
            out_weight.T,
            jnp.zeros((6, rows), BF16),
            up_weight.T,
            down_weight,
        ],
        0,
    )
    block = lax.all_gather(block, "row", axis=0).transpose(1, 0, 2).reshape(-1, full)
    attn_w = lax.all_gather(block[:144], COL, axis=0)
    up_w = lax.all_gather(block[144:280], XY, axis=0)
    down_w = lax.all_gather(block[280:], XY, axis=0)

    both = jnp.concatenate([layer_input, cotangent], 0).reshape(2 * width, 16, 256).transpose(1, 0, 2)
    got = lax.all_to_all(jnp.repeat(both, 2, axis=0), COL, split_axis=0, concat_axis=0, tiled=True)
    x_in = got[:, :width].reshape(full, 256).astype(F32)
    g_low = got[:, width:].reshape(full, 256)
    g = g_low.astype(F32)

    vectors = attn_w[:, 102, : 7 * width].reshape(32, 7, width).transpose(1, 0, 2).reshape(7, full, 1)
    vectors = vectors.astype(F32)
    q_bias, v_bias, o_bias, gain1, shift1, gain2, shift2 = (vectors[i] for i in range(7))
    hidden_bias = lax.dynamic_index_in_dim(
        attn_w[:, 103, :units].reshape(16, 2, units), core, 1, keepdims=False
    ).astype(F32)

    normed1, standard1, inv_std1 = norm(x_in, gain1, shift1)
    qkv = jnp.einsum("crd,dt->crt", attn_w[:, :102], normed1, preferred_element_type=F32)
    qkv = qkv.reshape(32, 3, width, 256).transpose(1, 0, 2, 3).reshape(3, full, 256)
    qkv = (qkv + jnp.stack([q_bias, jnp.zeros_like(q_bias), v_bias])).astype(BF16)

    seg = lax.dynamic_index_in_dim(segments, ix, 0, keepdims=False)
    seg_row, seg_col = seg[None], seg[:, None]
    count = jnp.where((iy == 0) & (core == 0), 3, 2).astype(jnp.int32).reshape(1)
    units_qkv = swap_heads(to_heads(qkv, core))
    units_out, lse = attend(count, units_qkv, seg_row, seg_col)
    attn = from_heads(units_out[:, None])[0]

    out_w = attn_w[:, 104:138]
    resid = (
        x_in
        + jnp.einsum("ced,dt->cet", out_w, attn, preferred_element_type=F32).reshape(full, 256)
        + o_bias
    )
    normed2, standard2, inv_std2 = norm(resid, gain2, shift2)
    hidden = jnp.einsum("xfd,dt->xft", up_w, normed2, preferred_element_type=F32) + hidden_bias[..., None]
    active, gelu_back = jax.vjp(lambda h: jax.nn.gelu(h, approximate=True), hidden)
    active = active.astype(BF16)
    down_part = jnp.einsum("xfd,xft->dt", down_w, active, preferred_element_type=F32)
    send_out = (down_part + jnp.where(core == 0, 1.0, 0.0) * resid).astype(BF16)
    got_out = lax.all_to_all(
        send_out.reshape(32, width, 256), COL, split_axis=0, concat_axis=0, tiled=True
    )
    layer_output = jnp.sum(got_out.reshape(16, 2, width, 256).astype(F32), 1)
    layer_output = layer_output.transpose(1, 0, 2).reshape(width, 4096)
    layer_output = layer_output + down_bias.astype(F32)[:, None]

    dactive = jnp.einsum("xfd,dt->xft", down_w, g_low, preferred_element_type=F32)
    dhidden = gelu_back(dactive)[0].astype(BF16)
    down_grad = jnp.einsum("xft,dt->xfd", active, g_low, preferred_element_type=F32).astype(BF16)
    up_grad = jnp.einsum("xft,dt->xfd", dhidden, normed2, preferred_element_type=F32).astype(BF16)
    upbias = jnp.sum(dhidden.astype(F32), -1)
    dn2 = jnp.einsum("xfd,xft->dt", up_w, dhidden, preferred_element_type=F32)
    dn2 = lax.psum(dn2, "core")
    back2, gain2_grad, shift2_grad = norm_back(dn2, standard2, inv_std2, gain2)
    dresid = g + back2
    dproj = dresid.astype(BF16)
    dattn = jnp.einsum(
        "ced,cet->dt", out_w, dproj.reshape(32, width, 256), preferred_element_type=F32
    ).astype(BF16)
    units_grad = swap_heads(to_heads(dattn[None], core))[:, 0]
    units_dqkv = attend_back(count, units_qkv, seg_row, seg_col, units_out, lse, units_grad)
    dqkv = from_heads(units_dqkv)
    by_block = dqkv.reshape(3, 32, width, 256).transpose(1, 0, 2, 3).reshape(32, 102, 256)
    dn1 = jnp.einsum("crd,crt->dt", attn_w[:, :102], by_block, preferred_element_type=F32)
    back1, gain1_grad, shift1_grad = norm_back(dn1, standard1, inv_std1, gain1)
    dqkv_sums = jnp.sum(dqkv.astype(F32), -1)
    vecs = jnp.stack(
        [
            dqkv_sums[0],
            dqkv_sums[2],
            jnp.sum(dproj.astype(F32), -1),
            jnp.sum(g, -1),
            gain1_grad,
            shift1_grad,
            gain2_grad,
            shift2_grad,
        ]
    ).reshape(8, 16, 2, width)
    vecs = lax.dynamic_index_in_dim(vecs, core, 2, keepdims=False).transpose(1, 0, 2).reshape(16, 8 * width)
    vecs = jnp.concatenate([vecs, upbias, jnp.zeros((16, 512 - 8 * width - units), F32)], 1)
    input_back = (dresid + back1).astype(BF16).reshape(16, 2, width, 256)
    input_back = lax.dynamic_index_in_dim(input_back, core, 1, keepdims=False)
    input_back = jnp.concatenate([input_back, vecs.astype(BF16).reshape(16, 2, 256)], 1)
    input_grad = lax.all_to_all(input_back, XY, split_axis=0, concat_axis=0, tiled=True)
    vecs = jnp.sum(input_grad[:, width:].reshape(16, 512).astype(F32), 0)
    vecs = lax.psum(vecs, "row")
    input_grad = input_grad[:, :width].transpose(1, 0, 2).reshape(width, 4096).astype(F32)

    mine = lax.dynamic_index_in_dim(by_block.reshape(16, 2, 102, 256), core, 1, keepdims=False)
    qkv_part = jnp.einsum("xrt,dt->xrd", mine, normed1, preferred_element_type=F32).astype(BF16)
    mine = lax.dynamic_index_in_dim(dproj.reshape(16, 2, width, 256), core, 1, keepdims=False)
    out_part = jnp.einsum("xrt,dt->xrd", mine, attn, preferred_element_type=F32).astype(BF16)
    attn_part = jnp.concatenate([qkv_part, out_part], 1)

    def scatter(part):
        return lax.psum_scatter(part, XY, scatter_dimension=0, tiled=False)

    sums = jnp.concatenate([scatter(attn_part), scatter(up_grad), scatter(down_grad)], 0)
    sums = sums.reshape(-1, 4, rows).transpose(1, 0, 2)
    sums = lax.psum_scatter(sums, "row", scatter_dimension=0, tiled=False).astype(F32)
    qkv_out = sums[:102].reshape(3, width, rows).transpose(2, 0, 1)
    out_out = sums[102:136].T
    up_out = sums[136:272].T
    down_out = sums[272:]

    small_out = vecs[: 8 * width].reshape(8, width)
    return (
        layer_output,
        input_grad,
        qkv_out,
        small_out[:2],
        out_out,
        small_out[2],
        up_out,
        vecs[8 * width : 8 * width + units],
        down_out,
        small_out[3],
        small_out[4],
        small_out[5],
        small_out[6],
        small_out[7],
    )


def solution(mesh):
    split = Mesh(mesh.devices.reshape(4, 4, 4, 2), ("row", "x", "y", "core"))
    vec = P(COL)
    return jax.shard_map(
        shards,
        mesh=split,
        in_specs=(
            P(COL, "row"),
            P(COL, "row"),
            P("row", None),
            P("row", None, COL),
            P(None, COL),
            P("row", COL),
            vec,
            P("row", COL),
            vec,
            P(COL, "row"),
            vec,
            vec,
            vec,
            vec,
            vec,
        ),
        out_specs=(
            P(COL, "row"),
            P(COL, "row"),
            P("row", None, COL),
            P(None, COL),
            P("row", COL),
            vec,
            P("row", COL),
            vec,
            P(COL, "row"),
            vec,
            vec,
            vec,
            vec,
            vec,
        ),
        check_vma=False,
    )
```

time: 1530 us -> 585 us (0.38)
  blocking collectives: 574 us -> 42.5 us
  local copies, waits for them, and re-layouts: 265 us -> 93 us
  waiting for transfers between devices: 386 us -> 300 us
  other arithmetic: 95.6 us -> 22.9 us
  matrix products: 116 us -> 57.8 us
  starting transfers between devices: 61.9 us -> 31.7 us
    unnamed x4 -> x0, blocking collectives: 509 us -> none
    unnamed x145 -> x100, local copies, waits for them, and re-layouts: 142 us -> 12.6 us
    unnamed x32 -> x11, waiting for transfers between devices: 226 us -> 120 us
    all_to_all x4 -> x6, waiting for transfers between devices: 37.6 us -> 112 us  [the longest x2 37.6 us: from_heads(): lax.all_to_all(send, ('y', 'core'), split_axis=0, concat_axis=0, tiled=True)]
    dot_general x54 -> x12, matrix products: 116 us -> 57.8 us  [the longest x1 8.48 us: shards(): jnp.einsum('crd,crt->dt', attn_w[:, :102], by_block, preferred_element_ty...]
    all_gather x4 -> x3, waiting for transfers between devices: 111 us -> 56.5 us  [the longest x1 32.6 us: shards(): attn_w = lax.all_gather(block[:144], COL, axis=0)]
    unnamed x21 -> x3, starting transfers between devices: 38.6 us -> 0.51 us
    all_gather x4 -> x1, blocking collectives: 54.3 us -> 16.9 us  [shards(): lax.all_gather(block, 'row', axis=0).transpose(1, 0, 2).reshape(-1, full)]
  transfers between devices with their start and end apart: 30 -> 14, of which waited for: 8 -> 11; matrix products, arithmetic and copies ran while one was open for 38% -> 25% of each run, Pallas kernels for 0% -> 2%
where the time goes in v1:
time: 585 us; the launch traced here: 575 us
  waiting for transfers between devices  300 us (51%)
  local copies, waits for them, and re-layouts  93 us (16%)
  matrix products  57.8 us (10%)
  blocking collectives  42.5 us (7%)
  starting transfers between devices  31.7 us (5%)
  other arithmetic  22.9 us (4%)
  between operations  15.7 us (3%)
  Pallas kernels  12.2 us (2%)
    unnamed x11, waiting for transfers between devices  120 us
    all_to_all x2, waiting for transfers between devices, from_heads(): lax.all_to_all(send, ('y', 'core'), split_axis=0, concat_axis=0, tiled=True)  37.6 us
    all_gather x1, waiting for transfers between devices, shards(): attn_w = lax.all_gather(block[:144], COL, axis=0)  32.6 us
    all_to_all x1, waiting for transfers between devices, swap_heads(): got = lax.all_to_all(send, 'y', split_axis=0, concat_axis=0, tiled=True)  29.2 us
    all_gather x1, waiting for transfers between devices, shards(): down_w = lax.all_gather(block[280:], XY, axis=0)  23.8 us
    all_to_all x1, waiting for transfers between devices, shards(): lax.all_to_all(jnp.repeat(both, 2, axis=0), COL, split_axis=0, concat_axi...  23.4 us
    all_gather x1, blocking collectives, shards(): lax.all_gather(block, 'row', axis=0).transpose(1, 0, 2).reshape(-1, full)  16.9 us
    all_to_all x1, blocking collectives, swap_heads(): got = lax.all_to_all(send, 'y', split_axis=0, concat_axis=0, tiled=True)  15 us
  transfers between devices with their start and end apart: 14, of which 11 were waited for; matrix products, arithmetic and copies ran while one was open for 25% of the time, Pallas kernels for 2%

profile of v1, /device:TPU:0, one launch (start us, length us, event | category | flops | bytes accessed | tf_op | source)
XLA Modules:
  0.0 575.4 jit_solution(8113527739809760048)
XLA Ops:
  13.2 16.9 %all-gather.1 = bf16[4,416,272]{1,2,0:T(8,128)(2,1)S(1)} all-gather(bf16[1,416,272]{1,2,0:T(8,128)(2,1)S(1)} %bitcast.197), channel_id=2, replica_groups=mesh['row'=4,'x'=4,'y'=4,'core'=2] {'row'}, dimensions={0}, use_global_device_ids=true | all-gather | bytes 1131520 | tf_op jit(solution)/shard_map/all_gather | solution.py:225
  35.2 7.3 %all-to-all-start = ((bf16[32,68,256]{2,1,0:T(8,128)(2,1)}), bf16[32,68,256]{2,1,0:T(8,128)(2,1)S(1)}, u32[]{:S(2)}, u32[]{:S(2)}) async-start(bf16[32,68,256]{2,1,0:T(8,128)(2,1)} %bitcast.13), calls=%async_computation | async-start | bytes 2359296 | tf_op jit(solution)/shard_map/all_to_all | solution.py:231
  42.6 23.4 %all-to-all-done = bf16[32,68,256]{2,1,0:T(8,128)(2,1)S(1)} async-done(((bf16[32,68,256]{2,1,0:T(8,128)(2,1)}), bf16[32,68,256]{2,1,0:T(8,128)(2,1)S(1)}, u32[]{:S(2)}, u32[]{:S(2)}) %all-to-all-start) | async-done | bytes 1114144 | tf_op jit(solution)/shard_map/all_to_all | solution.py:231
  66.6 32.6 %all-gather.10.cloned.1.call-done = bf16[32,144,1088]{2,1,0:T(8,128)(2,1)} async-done(((bf16[1,144,1088]{2,1,0:T(8,128)(2,1)}), bf16[32,144,1088]{2,1,0:T(8,128)(2,1)}) %all-gather.10.cloned.1.call-update) | async-done | bytes 10027024 | tf_op jit(solution)/shard_map/all_gather | solution.py:226
  100.3 3.2 slice-done
  103.5 4.0 copy.115
  108.4 6.9 %fusion.13 = f32[3,32,34,256]{3,2,0,1:T(8,128)S(1)} fusion(bf16[32,3,34,1088]{3,0,2,1:T(8,128)(2,1)} %bitcast.171, bf16[1088,256,1,1]{1,0,2,3:T(8,128)(2,1)S(1)} %reshape.350), kind=kOutput, calls=%fused_computation.28 | convolution fusion | flops 1818230784 | bytes 11001856 | tf_op jit(solution)/shard_map/crd,dt->crt/dot_general | solution.py:244
  115.3 2.3 copy.117
  117.6 4.7 reshape.324
  122.7 2.4 fusion.17
  126.5 4.0 all-to-all-start.1
  130.7 29.2 %all-to-all-done.1 = bf16[4,3,3,64,256]{4,3,2,1,0:T(8,128)(2,1)S(1)} async-done(((bf16[4,3,3,64,256]{4,3,2,1,0:T(8,128)(2,1)}), bf16[4,3,3,64,256]{4,3,2,1,0:T(8,128)(2,1)S(1)}, u32[]{:S(2)}, u32[]{:S(2)}) %all-to-all-start.1) | async-done | bytes 1179680 | tf_op jit(solution)/shard_map/all_to_all | solution.py:173
  160.9 1.4 copy.158
  162.4 5.9 %shard_map.254 = (bf16[3,64,1024]{2,1,0:T(8,128)(2,1)S(1)}, f32[3,1,1024]{2,1,0:T(1,128)S(1)}) custom-call(s32[1]{0:T(128)} %bitcast.15.count_ref, bf16[3,3,64,1024]{3,2,1,0:T(8,128)(2,1)S(1)} %bitcast.166, s32[1,1024]{1,0:T(1,128)S(1)} %constant_dynamic-slice_fusion.3.seg_row_ref, s32[1024,1]{1,0:T(8,128)S(1)} %copy.122.seg_col_ref), custom_call_target="tpu_custom_call" | custom-call | tf_op jit(solution)/shard_map/pallas_call | solution.py:109
  171.3 4.7 all-to-all-start.2
  176.1 1.6 fusion.33
  177.7 2.5 reshape.341
  181.3 3.6 slice.213
  184.9 4.6 dot_general.40
  190.8 2.3 all-to-all-done.2
  193.1 1.3 copy.124
  194.6 2.7 fusion.37
  197.5 5.9 %fusion.27 = f32[16,136,256]{2,1,0:T(8,128)} fusion(bf16[16,136,1088]{2,1,0:T(8,128)(2,1)} %all-gather.8.cloned.1.call-done, f32[1088,256]{1,0:T(8,128)S(1)} %get-tuple-element.81, f32[1088]{0:T(1024)S(1)} %add.143, f32[1088]{0:T(1024)S(1)} %mul.166, f32[256]{0:T(256)S(1)} %add_rsqrt_fusion, f32[256]{0:T(256)S(1)} %broadcast_multiply_fusion.4), kind=kOutput, calls=%fused_computation.110 | convolution fusion | flops 1213546496 | bytes 8088064 | tf_op jit(solution)/shard_map/xfd,dt->xft/dot_general | solution.py:262
  203.4 23.8 %all-gather.6.cloned.1.call-done = bf16[16,136,1088]{2,1,0:T(8,128)(2,1)} async-done(((bf16[1,136,1088]{2,1,0:T(8,128)(2,1)}), bf16[16,136,1088]{2,1,0:T(8,128)(2,1)}) %all-gather.6.cloned.1.call-update) | async-done | bytes 4734992 | tf_op jit(solution)/shard_map/all_gather | solution.py:228
  227.2 7.1 %fusion.38 = (bf16[16,136]{1,0:T(8,128)(2,1)}, bf16[16,136,256]{2,1,0:T(8,128)(2,1)S(1)}) fusion(f32[16,136,256]{2,1,0:T(8,128)} %fusion.27, f32[16,136]{1,0:T(8,128)S(1)} %bitcast.213, bf16[16,136,1088]{2,1,0:T(8,128)(2,1)} %all-gather.6.cloned.1.call-done, bf16[1088,256,1]{1,0,2:T(8,128)(2,1)} %reshape.353), kind=kOutput, calls=%fused_computation.119 | convolution fusion | flops 1224406912 | bytes 8647424 | tf_op jit(solution)/shard_map/xfd,dt->xft/dot_general | solution.py:274
  235.3 2.6 convolution_bitcast_fusion.2
  238.0 6.3 %convolution_convert_fusion = bf16[16,136,1088]{2,1,0:T(8,128)(2,1)} fusion(bf16[1088,256,1]{1,0,2:T(8,128)(2,1)} %reshape.353, f32[16,136,256]{2,1,0:T(8,128)} %fusion.27, f32[16,136]{1,0:T(8,128)S(1)} %bitcast.214), kind=kOutput, calls=%fused_computation.2 | convolution fusion | flops 1220091904 | bytes 7528960 | tf_op jit(solution)/shard_map/xft,dt->xfd/dot_general | solution.py:276
  244.5 5.3 convolution_convert_fusion.1
  249.8 2.0 reshape.330
  251.8 11.2 %all-reduce.7.cloned.1.call-done = f32[1088,256]{1,0:T(8,128)} async-done(((f32[1088,256]{1,0:T(8,128)}), f32[1088,256]{1,0:T(8,128)}) %all-reduce.7.cloned.1.call-update) | async-done | bytes 1114128 | tf_op jit(solution)/shard_map/psum | solution.py:280
  263.1 2.0 multiply_reduce_fusion.1
  265.1 1.9 convert_reduce_fusion.3
  267.0 1.2 reshape.331
  268.2 2.8 fusion.4
  271.2 15.0 %all_to_all.35 = bf16[4,3,1,64,256]{4,3,1,2,0:T(8,128)(2,1)S(1)} all-to-all(bf16[4,3,1,64,256]{4,3,1,2,0:T(8,128)(2,1)S(1)} %pad_maximum_fusion.3), channel_id=1, replica_groups=mesh['row'=4,'x'=4,'y'=4,'core'=2] {'y'}, dimensions={0} | all-to-all | bytes 786432 | tf_op jit(solution)/shard_map/all_to_all | solution.py:173
  288.5 6.4 %shard_map.255 = bf16[3,3,64,1024]{3,2,1,0:T(8,128)(2,1)S(1)} custom-call(s32[1]{0:T(128)} %bitcast.15.count_ref, bf16[3,3,64,1024]{3,2,1,0:T(8,128)(2,1)S(1)} %bitcast.167, s32[1,1024]{1,0:T(1,128)S(1)} %constant_dynamic-slice_fusion.3.seg_row_ref, s32[1024,1]{1,0:T(8,128)S(1)} %copy.122.seg_col_ref, bf16[3,64,1024]{2,1,0:T(8,128)(2,1)S(1)} %get-tuple-element.16.out_ref, ...), custom_call_target="tpu_custom_call" | custom-call | tf_op jit(solution)/shard_map/pallas_call | solution.py:129
  296.0 1.8 broadcast_in_dim.40
  297.8 4.5 all-to-all-start.5
  303.7 1.8 convolution_convert_fusion.3
  305.5 35.3 %all-to-all-done.5 = bf16[8,3,3,64,256]{4,3,1,2,0:T(8,128)(2,1)} async-done(((bf16[8,3,3,64,256]{4,3,1,2,0:T(8,128)(2,1)}), bf16[8,3,3,64,256]{4,3,1,2,0:T(8,128)(2,1)}, u32[]{:S(2)}, u32[]{:S(2)}) %all-to-all-start.5) | async-done | bytes 2359328 | tf_op jit(solution)/shard_map/all_to_all | solution.py:182
  340.8 1.8 copy.130
  342.6 1.3 slice.230
  344.0 3.7 reshape_reshape.6
  347.6 3.1 copy.131
  350.8 4.6 reshape_reshape.7
  355.3 3.5 constant_dynamic-slice_fusion
  358.8 2.0 convolution_convert_fusion.2
  360.9 2.9 pad_maximum_fusion
  363.8 1.2 copy-done.4
  365.0 6.0 %fusion.5 = bf16[1088,256]{1,0:T(8,128)(2,1)} fusion(bf16[16,136,1088]{2,1,0:T(8,128)(2,1)} %all-gather.6.cloned.1.call-done, f32[1088,256]{1,0:T(8,128)S(1)} %copy-done.4, f32[]{:T(128)S(6)} %select_n.30, f32[16,136,256]{2,1,0:T(8,128)} %fusion.27, f32[16,136]{1,0:T(8,128)S(1)} %bitcast.215), kind=kOutput, calls=%fused_computation.19 | convolution fusion | flops 1218560000 | bytes 8643076 | tf_op jit(solution)/shard_map/xfd,xft->dt/dot_general | solution.py:265
  371.0 2.0 reshape.328
  373.0 5.4 all-to-all-start.3
  380.0 14.0 %all-to-all-done.3 = bf16[32,34,256]{2,1,0:T(8,128)(2,1)} async-done(((bf16[32,34,256]{2,1,0:T(8,128)(2,1)}), bf16[32,34,256]{2,1,0:T(8,128)(2,1)}, u32[]{:S(2)}, u32[]{:S(2)}) %all-to-all-start.3) | async-done | bytes 557088 | tf_op jit(solution)/shard_map/all_to_all | solution.py:267
  394.0 1.3 convert_reduce_fusion.1
  395.6 1.2 copy.160
  398.0 8.5 %multiply_reduce_fusion.3 = (f32[256]{0:T(256)S(1)}, bf16[1088]{0:T(1024)(128)(2,1)S(1)}, f32[256]{0:T(256)S(1)}, bf16[1088]{0:T(1024)(128)(2,1)S(1)}, f32[1088,256]{1,0:T(8,128)}) fusion(f32[1088,256]{1,0:T(8,128)} %reshape.341, f32[256]{0:T(256)} %copy-done.27, f32[1088]{0:T(1024)S(1)} %mul.192, f32[256]{0:T(256)} %copy-done.33, ...), kind=kOutput, calls=%fused_computation.41 | convolution fusion | flops 1820734976 | bytes 11579904 | tf_op jit(solution)/shard_map/crd,crt->dt/dot_general | solution.py:291
  407.1 2.3 add_convert_fusion.2
  410.6 37.3 %reduce-scatter.15.cloned.1.call-done = bf16[1,136,1088]{2,1,0:T(8,128)(2,1)} async-done(((bf16[16,136,1088]{2,1,0:T(8,128)(2,1)}), bf16[1,136,1088]{2,1,0:T(8,128)(2,1)}) %reduce-scatter.15.cloned.1.call-update) | async-done | bytes 295952
  449.1 82.4 %reduce-scatter.13.cloned.1.call-done = bf16[1,136,1088]{2,1,0:T(8,128)(2,1)} async-done(((bf16[16,136,1088]{2,1,0:T(8,128)(2,1)}), bf16[1,136,1088]{2,1,0:T(8,128)(2,1)}) %reduce-scatter.13.cloned.1.call-update) | async-done | bytes 295952
  532.7 1.6 maximum_bitcast_fusion
  535.6 4.8 all-to-all-start.6
  541.5 7.8 %all-to-all-done.6 = bf16[16,36,256]{2,1,0:T(8,128)(2,1)S(1)} async-done(((bf16[16,36,256]{2,1,0:T(8,128)(2,1)}), bf16[16,36,256]{2,1,0:T(8,128)(2,1)S(1)}, u32[]{:S(2)}, u32[]{:S(2)}) %all-to-all-start.6) | async-done | bytes 294944 | tf_op jit(solution)/shard_map/all_to_all | solution.py:311
  549.3 10.7 %psum.15 = f32[512]{0:T(512)S(1)} all-reduce(f32[512]{0:T(512)S(1)} %bitcast.217), channel_id=1, replica_groups=mesh['row'=4,'x'=4,'y'=4,'core'=2] {'row'}, use_global_device_ids=true, to_apply=%region_23.24 | all-reduce | flops 512 | bytes 4096 | tf_op jit(solution)/shard_map/psum | solution.py:313
  561.0 1.2 copy.161
  (227 shorter events, 44.8 us)
Async XLA Ops:
  7.2 123.3 %copy-start = (s32[4,1024]{1,0:T(4,128)S(1)}, s32[4,1024]{1,0:T(4,128)}, u32[]{:S(2)}) copy-start(s32[4,1024]{1,0:T(4,128)} %param.17) | copy-start | bytes 49156
  7.2 92.0 %all-gather.10.cloned.1.call-start = ((), (), s32[]{:S(2)}) async-start(), calls=%async_computation.13 | async-start | bytes 10948608 | tf_op jit(solution)/shard_map/all_gather | solution.py:226
  31.1 166.4 %all-gather.8.cloned.1.call-start = ((), (), s32[]{:S(2)}) async-start(), calls=%async_computation.12 | async-start | bytes 5326848 | tf_op jit(solution)/shard_map/all_gather | solution.py:227
  31.6 2.0 copy-start.22
  31.6 2.0 copy-start.23
  32.6 194.7 %all-gather.6.cloned.1.call-start = ((), (), s32[]{:S(2)}) async-start(), calls=%async_computation.11 | async-start | bytes 5326848 | tf_op jit(solution)/shard_map/all_gather | solution.py:228
  35.2 30.8 %all-to-all-start = ((bf16[32,68,256]{2,1,0:T(8,128)(2,1)}), bf16[32,68,256]{2,1,0:T(8,128)(2,1)S(1)}, u32[]{:S(2)}, u32[]{:S(2)}) async-start(bf16[32,68,256]{2,1,0:T(8,128)(2,1)} %bitcast.13), calls=%async_computation | async-start | bytes 2359296 | tf_op jit(solution)/shard_map/all_to_all | solution.py:231
  66.2 41.6 %copy-start.27 = (f32[256]{0:T(256)}, f32[256]{0:T(256)S(1)}, u32[]{:S(2)}) copy-start(f32[256]{0:T(256)S(1)} %broadcast_multiply_fusion.5) | copy-start | bytes 3076
  66.6 41.2 %copy-start.33 = (f32[256]{0:T(256)}, f32[256]{0:T(256)S(1)}, u32[]{:S(2)}) copy-start(f32[256]{0:T(256)S(1)} %add_rsqrt_fusion.1) | copy-start | bytes 3076
  100.3 3.2 slice-start
  108.2 7.1 %copy-start.8 = (bf16[32,34,256]{2,1,0:T(8,128)(2,1)}, bf16[32,34,256]{2,1,0:T(8,128)(2,1)S(1)}, u32[]{:S(2)}) copy-start(bf16[32,34,256]{2,1,0:T(8,128)(2,1)S(1)} %add_convert_fusion.1) | copy-start | bytes 1671172
  126.5 33.4 %all-to-all-start.1 = ((bf16[4,3,3,64,256]{4,3,2,1,0:T(8,128)(2,1)}), bf16[4,3,3,64,256]{4,3,2,1,0:T(8,128)(2,1)S(1)}, u32[]{:S(2)}, u32[]{:S(2)}) async-start(bf16[4,3,3,64,256]{4,3,2,1,0:T(8,128)(2,1)} %pad_maximum_fusion.1), calls=%async_computation.1 | async-start | bytes 2359296 | tf_op jit(solution)/shard_map/all_to_all | solution.py:173
  159.9 1.0 copy-start.14
  171.3 21.7 %all-to-all-start.2 = ((bf16[8,3,1,64,256]{4,3,1,2,0:T(8,128)(2,1)}), bf16[8,3,1,64,256]{4,3,1,2,0:T(8,128)(2,1)}, u32[]{:S(2)}, u32[]{:S(2)}) async-start(bf16[8,3,1,64,256]{4,3,1,2,0:T(8,128)(2,1)} %bitcast.178), calls=%async_computation.2 | async-start | bytes 1572864 | tf_op jit(solution)/shard_map/all_to_all | solution.py:182
  176.0 87.0 %all-reduce.7.cloned.1.call-start = ((), (), s32[]{:S(2)}) async-start(), calls=%async_computation.14 | async-start | bytes 2228224 | tf_op jit(solution)/shard_map/psum | solution.py:280
  177.7 2.5 copy-start.10
  190.8 47.2 %copy-start.25 = (f32[16,1,136]{2,0,1:T(8,128)}, f32[16,1,136]{2,0,1:T(8,128)S(1)}, u32[]{:S(2)}) copy-start(f32[16,1,136]{2,0,1:T(8,128)S(1)} %copy.184) | copy-start | bytes 26116
  193.1 1.5 copy-start.15
  194.4 2.9 copy-start.17
  197.3 67.8 %copy-start.3 = (f32[1088,256]{1,0:T(8,128)}, f32[1088,256]{1,0:T(8,128)S(1)}, u32[]{:S(2)}) copy-start(f32[1088,256]{1,0:T(8,128)S(1)} %get-tuple-element.81) | copy-start | bytes 3342340
  227.2 8.1 %copy-start.38 = (bf16[16,136,1088]{2,1,0:T(8,128)(2,1)S(1)}, bf16[16,136,1088]{2,1,0:T(8,128)(2,1)}, u32[]{:S(2)}) copy-start(bf16[16,136,1088]{2,1,0:T(8,128)(2,1)} %all-gather.8.cloned.1.call-done) | copy-start | bytes 14204932
  234.3 1.0 copy-start.20
  237.9 171.5 %reduce-scatter.17.cloned.1.call-start = ((), (), s32[]{:S(2)}) async-start(), calls=%async_computation.18 | async-start | bytes 5326848
  244.3 203.6 %reduce-scatter.15.cloned.1.call-start = ((), (), s32[]{:S(2)}) async-start(), calls=%async_computation.17 | async-start | bytes 5326848
  263.1 2.1 copy-start.5
  263.1 2.1 copy-start.12
  265.1 1.9 copy-start.29
  265.1 1.9 copy-start.31
  287.5 1.0 copy-start.2
  297.8 4.8 copy-start.9
  297.8 43.0 %all-to-all-start.5 = ((bf16[8,3,3,64,256]{4,3,1,2,0:T(8,128)(2,1)}), bf16[8,3,3,64,256]{4,3,1,2,0:T(8,128)(2,1)}, u32[]{:S(2)}, u32[]{:S(2)}) async-start(bf16[8,3,3,64,256]{4,3,1,2,0:T(8,128)(2,1)} %bitcast.48), calls=%async_computation.5 | async-start | bytes 4718592 | tf_op jit(solution)/shard_map/all_to_all | solution.py:182
  302.3 1.3 copy-start.11
  302.3 1.4 copy-start.18
  302.3 229.2 %reduce-scatter.13.cloned.1.call-start = ((), (), s32[]{:S(2)}) async-start(), calls=%async_computation.16 | async-start | bytes 5326848
  355.3 3.5 copy-start.19
  358.8 2.0 copy-start.7
  363.8 1.2 copy-start.4
  363.8 1.2 copy-start.26
  371.0 7.7 %copy-start.39 = (bf16[34]{0:T(256)(128)(2,1)S(1)}, bf16[34]{0:T(256)(128)(2,1)}, u32[]{:S(2)}) copy-start(bf16[34]{0:T(256)(128)(2,1)} %param.25) | copy-start | bytes 208
  373.0 21.0 %all-to-all-start.3 = ((bf16[32,34,256]{2,1,0:T(8,128)(2,1)}), bf16[32,34,256]{2,1,0:T(8,128)(2,1)}, u32[]{:S(2)}, u32[]{:S(2)}) async-start(bf16[32,34,256]{2,1,0:T(8,128)(2,1)} %reshape.328), calls=%async_computation.3 | async-start | bytes 1310720 | tf_op jit(solution)/shard_map/all_to_all | solution.py:267
  378.4 185.0 %reduce-scatter.11.cloned.1.call-start = ((), (), s32[]{:S(2)}) async-start(), calls=%async_computation.15 | async-start | bytes 1392640 | tf_op jit(solution)/shard_map/reduce_scatter | solution.py:327
  395.5 1.3 copy-start.24
  397.9 9.2 %copy-start.6 = (f32[1088,256]{1,0:T(8,128)S(1)}, f32[1088,256]{1,0:T(8,128)}, u32[]{:S(2)}) copy-start(f32[1088,256]{1,0:T(8,128)} %all-reduce.7.cloned.1.call-done) | copy-start | bytes 3342340
  397.9 9.2 %copy-start.13 = (bf16[1088,256]{1,0:T(8,128)(2,1)S(1)}, bf16[1088,256]{1,0:T(8,128)(2,1)}, u32[]{:S(2)}) copy-start(bf16[1088,256]{1,0:T(8,128)(2,1)} %reshape.330) | copy-start | bytes 1671172
  397.9 9.2 %copy-start.28 = (f32[256]{0:T(256)S(1)}, f32[256]{0:T(256)}, u32[]{:S(2)}) copy-start(f32[256]{0:T(256)} %copy-done.27) | copy-start | bytes 3076
  398.0 9.2 %copy-start.30 = (f32[256]{0:T(256)S(1)}, f32[256]{0:T(256)}, u32[]{:S(2)}) copy-start(f32[256]{0:T(256)} %copy-done.29) | copy-start | bytes 3076
  398.0 9.2 %copy-start.32 = (f32[256]{0:T(256)S(1)}, f32[256]{0:T(256)}, u32[]{:S(2)}) copy-start(f32[256]{0:T(256)} %copy-done.31) | copy-start | bytes 3076
  398.0 9.2 %copy-start.34 = (f32[256]{0:T(256)S(1)}, f32[256]{0:T(256)}, u32[]{:S(2)}) copy-start(f32[256]{0:T(256)} %copy-done.33) | copy-start | bytes 3076
  532.7 1.7 copy-start.35
  532.7 1.7 copy-start.36
  534.7 5.8 %copy-start.16 = (f32[5,8,16,256]{3,1,2,0:T(8,128)S(1)}, f32[5,8,16,256]{3,1,2,0:T(8,128)}, u32[]{:S(2)}) copy-start(f32[5,8,16,256]{3,1,2,0:T(8,128)} %copy.160) | copy-start | bytes 1966084
  534.7 5.8 %copy-start.37 = (f32[34]{0:T(128)S(1)}, f32[34]{0:T(128)}, u32[]{:S(2)}) copy-start(f32[34]{0:T(128)} %convert_element_type.151) | copy-start | bytes 412
  535.6 13.7 %all-to-all-start.6 = ((bf16[16,36,256]{2,1,0:T(8,128)(2,1)}), bf16[16,36,256]{2,1,0:T(8,128)(2,1)S(1)}, u32[]{:S(2)}, u32[]{:S(2)}) async-start(bf16[16,36,256]{2,1,0:T(8,128)(2,1)} %copy.136), calls=%async_computation.6 | async-start | bytes 655360 | tf_op jit(solution)/shard_map/all_to_all | solution.py:311
  563.4 1.4 copy-start.21
  564.6 3.5 copy-start.1
Sparse Core Ops, SparseCore 0:
  31.2 67.9 all-gather.9
  101.4 66.3 all-gather.7
  170.0 57.2 all-gather.5
  238.1 24.9 all-reduce.6
  266.7 94.0 reduce-scatter.16
  364.2 83.6 reduce-scatter.14
  451.8 79.6 reduce-scatter.12
  534.5 23.3 reduce-scatter.10
